TPU v7x, 32 devices: a whole 2x2x4 slice. The times are simulated.
32 devices in a mesh: slab: 8 (over z, x), tile: 4 (over y, core).
Axes of the slice: x: 2, y: 2, z: 4, core: 2. Of those that a mesh axis runs over, the one named last changes fastest.
Arguments:
- old_fine: float32 [2048, 5, 512], P(('slab', 'tile')), may hold values from -6 to 6
- coarse_fine: float32 [2048, 5, 64], P(('slab', 'tile')), may hold values from -6 to 6
- old_owner: int32 [8, 4, 64], P('slab', 'tile'), may hold values from 0 to 3, as said below
- new_refine: int32 [8, 4, 64], P('slab', 'tile'), may hold values from 0 to 1
- parent_map: int32 [8, 4, 64], P('slab', 'tile'), may hold values from 0 to 63
- courant: float32 [3, 5], replicated, may hold values from 0.05 to 0.3
Outputs:
- fine_next: float32 [5, 64, 128, 128], P(None, 'slab', 'tile')
Inputs may be any that keep to these rules, and one draw needn't show every extreme that they name: `old_owner`: in each slab, old block k of tile t goes to tile (t + o_k) mod 4 with offsets o_k of the slab; every device sends exactly 16 blocks to each tile, and new slot k receives old slot k.
All inputs are finite; a program needn't handle non-finite values.
Results may differ from a plain program's by a relative error of at most 0.0003.
Values sent between devices are 32-bit elements; how exact they have to be, the bound alone decides.
A program may use at most 64 MiB of HBM per device.

v0:
```python
import jax
import jax.numpy as jnp
from jax import lax
from jax.sharding import PartitionSpec as P

E = 8
BX = 16
BY = 4


def shifted_2(x, axis, by):
    peers = lax.axis_size(axis)
    return lax.ppermute(x, axis, [(i, (i + by) % peers) for i in range(peers)])


def with_halo(block, sides, width):
    for axis, dim in sides:
        count = lax.axis_size(axis)
        forward = [(i, i + 1) for i in range(count - 1)]
        backward = [(target, source) for source, target in forward]
        low = lax.ppermute(
            lax.slice_in_dim(block, block.shape[dim] - width, None, axis=dim), axis, forward
        )
        high = lax.ppermute(lax.slice_in_dim(block, 0, width, axis=dim), axis, backward)
        block = jnp.concatenate([low, block, high], axis=dim)
    return block


def minmod(left, right):
    return 0.5 * (jnp.sign(left) + jnp.sign(right)) * jnp.minimum(jnp.abs(left), jnp.abs(right))


def slopes(cells, axis):
    width = [(0, 0)] * cells.ndim
    width[axis] = (1, 1)
    padded = jnp.pad(cells, width, mode="edge")
    size = cells.shape[axis]
    below = lax.slice_in_dim(padded, 0, size, axis=axis)
    above = lax.slice_in_dim(padded, 2, size + 2, axis=axis)
    return minmod(cells - below, above - cells)


def refine_block(cells):
    nd = cells.ndim
    slope_z = slopes(cells, nd - 3)
    slope_y = slopes(cells, nd - 2)
    slope_x = slopes(cells, nd - 1)
    sigma = jnp.array([-0.25, 0.25], jnp.float32)

    def spread(value):
        return value[..., :, None, :, None, :, None]

    offset = (
        spread(slope_z) * sigma[:, None, None, None, None]
        + spread(slope_y) * sigma[:, None, None]
        + spread(slope_x) * sigma
    )
    fine = spread(cells) + offset
    half = cells.shape[-1]
    return fine.reshape(cells.shape[:-3] + (2 * half, 2 * half, 2 * half))


def advance(padded, courant):
    fields, zp, yp, xp = padded.shape
    zn, yn, xn = (zp - 4, yp - 4, xp - 4)

    def cut(dz, dy, dx):
        return padded[:, 2 + dz : 2 + dz + zn, 2 + dy : 2 + dy + yn, 2 + dx : 2 + dx + xn]

    center = cut(0, 0, 0)
    total = jnp.zeros_like(center)
    for axis, unit in enumerate(((1, 0, 0), (0, 1, 0), (0, 0, 1))):
        lower1 = cut(-unit[0], -unit[1], -unit[2])
        lower2 = cut(-2 * unit[0], -2 * unit[1], -2 * unit[2])
        upper1 = cut(unit[0], unit[1], unit[2])
        face_hi = center + 0.5 * minmod(center - lower1, upper1 - center)
        face_lo = lower1 + 0.5 * minmod(lower1 - lower2, center - lower1)
        total = total + courant[axis][:, None, None, None] * (face_hi - face_lo)
    return center - total


def local(old_fine, coarse_fine, old_owner, new_refine, parent_map, courant):
    tiles = lax.axis_size("tile")
    myself = lax.axis_index("tile")
    blocks, fields, cells = old_fine.shape
    per_peer = blocks // tiles
    half = E // 2
    owner = old_owner.reshape(-1)
    send_order = jnp.argsort(owner, stable=True)
    outgoing = old_fine[send_order].reshape(tiles, per_peer, fields, cells)
    arrived = lax.all_to_all(outgoing, "tile", split_axis=0, concat_axis=0, tiled=True).reshape(
        blocks, fields, cells
    )
    source = (2 * myself - owner) % tiles
    recv_order = jnp.argsort(source, stable=True)
    moved = arrived[jnp.argsort(recv_order)]
    parents = parent_map.reshape(-1)
    shifted = shifted_2(coarse_fine, "slab", 1)
    filled = refine_block(shifted[parents].reshape(blocks, fields, half, half, half)).reshape(
        blocks, fields, cells
    )
    flags = new_refine.reshape(-1)
    refilled = jnp.where((flags == 1)[:, None, None], filled, moved)
    region = (
        refilled.reshape(BY, BX, fields, E, E, E)
        .transpose(2, 3, 0, 4, 1, 5)
        .reshape(fields, E, BY * E, BX * E)
    )
    padded = with_halo(region, (("slab", 1), ("tile", 2)), 2)
    padded = jnp.pad(padded, ((0, 0), (0, 0), (0, 0), (2, 2)))
    return advance(padded, courant)


def solution(mesh):
    in_specs = (
        P(("slab", "tile"), None, None),
        P(("slab", "tile"), None, None),
        P("slab", "tile", None),
        P("slab", "tile", None),
        P("slab", "tile", None),
        P(),
    )
    out_specs = P(None, "slab", "tile", None)
    return jax.shard_map(local, mesh=mesh, in_specs=in_specs, out_specs=out_specs, check_vma=False)
```

profile of v0, /device:TPU:1, one launch (start us, length us, event | category | flops | bytes accessed | tf_op | source)
XLA Modules:
  0.0 83.2 jit_solution(13552131971322706473)
XLA Ops:
  0.0 0.0 copy-start
  0.0 1.1 %copy.17 = f32[64,5,64]{2,1,0:T(8,128)S(1)} copy(f32[64,5,64]{2,0,1:T(8,128)} %param.8) | data formatting | bytes 163840 | tf_op args[1]
  1.1 2.1 %collective-permute-start = (f32[64,5,64]{2,1,0:T(8,128)S(1)}, f32[64,5,64]{2,1,0:T(8,128)S(1)}, u32[]{:S(2)}, u32[]{:S(2)}) collective-permute-start(f32[64,5,64]{2,1,0:T(8,128)S(1)} %copy.17), channel_id=1, source_target_pairs={{0,4},{4,8},{8,12},{12,16},{16,20},{20,24},{24,28},{28,0},{1,5},{5... | collective-permute-start | bytes 245768 | tf_op jit(solution)/shard_map/ppermute | solution.py:13
  3.2 2.7 %sort.48 = (s32[64]{0:T(128)}, s32[64]{0:T(128)S(1)}) sort(s32[64]{0:T(128)} %bitcast.30, s32[64]{0:T(128)S(1)} %iota.11), dimensions={0}, to_apply=%region_0.0 | sort | flops 384 | bytes 1024 | tf_op jit(solution)/shard_map/jit(argsort)/sort | solution.py:89
  5.9 0.0 copy-done
  5.9 1.5 %gather_fusion.1 = f32[64,5,512]{2,0,1:T(8,128)S(1)} fusion(f32[64,5,512]{2,0,1:T(8,128)S(1)} %copy-done, s32[1024]{0:T(1024)S(1)} %pad_clamp_fusion.1), kind=kCustom, calls=%fused_computation.1 | custom fusion | bytes 1310976 | tf_op jit(solution)/shard_map/gather | solution.py:90
  7.4 0.0 copy-start.3
  7.5 0.0 copy-start.4
  7.5 0.0 copy-start.5
  7.5 0.0 copy-start.1
  7.5 0.9 %copy.19 = f32[4,16,5,512]{3,1,2,0:T(8,128)} copy(f32[4,16,5,512]{3,1,0,2:T(8,128)S(1)} %bitcast.23) | data formatting | bytes 1310720 | tf_op jit(solution)/shard_map/reshape | solution.py:90
  8.4 4.4 %all-to-all-start = ((f32[4,16,5,512]{3,1,2,0:T(8,128)}), f32[4,16,5,512]{3,1,2,0:T(8,128)S(1)}, u32[]{:S(2)}, u32[]{:S(2)}) async-start(f32[4,16,5,512]{3,1,2,0:T(8,128)} %copy.19), calls=%async_computation | async-start | bytes 1310720 | tf_op jit(solution)/shard_map/all_to_all | solution.py:91
  12.8 0.0 copy-done.3
  12.8 0.0 copy-done.4
  12.8 2.1 %sort.49 = (s32[64]{0:T(128)}, s32[64]{0:T(128)S(1)}) sort(s32[64]{0:T(128)S(1)} %and_select_fusion, s32[64]{0:T(128)S(1)} %iota.12), dimensions={0}, to_apply=%region_1.2 | sort | flops 384 | bytes 1024 | tf_op jit(solution)/shard_map/jit(argsort)/sort | solution.py:95
  15.0 2.1 %sort.50 = (s32[64]{0:T(128)}, s32[64]{0:T(128)S(1)}) sort(s32[64]{0:T(128)S(1)} %get-tuple-element.9, s32[64]{0:T(128)S(1)} %iota.13), dimensions={0}, to_apply=%region_2.3 | sort | flops 384 | bytes 1024 | tf_op jit(solution)/shard_map/jit(argsort)/sort | solution.py:96
  17.1 0.1 eq.17
  17.2 0.0 collective-permute-done
  17.2 0.6 gather_fusion
  17.8 0.1 copy.18
  18.0 0.1 fusion.17
  18.1 0.9 %minimum_multiply_fusion.2 = (f32[64,5,4,4,4]{0,4,3,2,1:T(4,128)S(1)}, f32[64,5,4,4,4]{0,4,3,2,1:T(4,128)S(1)}, f32[64,5,4,4,4]{0,4,3,2,1:T(4,128)S(1)}) fusion(f32[64,5,4,4,4]{0,4,3,2,1:T(4,128)S(1)} %bitcast.28, f32[64,5,1,4,4]{0,4,3,2,1:T(4,128)S(1)} %get-tuple-element.23, f32[64,5,1,4,4]{0,4,3,2,1:T(4,128)S(1)} %get-tuple-element.22, ...), kind=kLoop, calls=%fused_computation.41 | loop fusion | flops 737280 | bytes 450560 | tf_op jit(solution)/shard_map/mul | solution.py:30
  19.1 0.1 broadcast_multiply_fusion.1
  19.2 0.1 broadcast_multiply_fusion.2
  19.3 0.2 broadcast_add_fusion
  19.5 0.2 broadcast_multiply_fusion
  19.8 0.8 add_add_fusion
  20.6 4.6 %add.137 = f32[4,16,5,8,8,8]{1,0,5,4,3,2:T(4,128)} reshape(f32[64,5,4,2,4,2,4,2]{0,7,6,5,4,3,2,1:T(2,128)S(1)} %add_add_fusion) | data formatting | bytes 1310720 | tf_op jit(solution)/shard_map/add | solution.py:58
  25.2 0.0 all-to-all-done
  25.2 0.4 copy.20
  25.6 0.6 gather_fusion.2
  26.3 0.5 copy.21
  26.8 3.8 %gather.14 = f32[4,16,5,8,8,8]{1,0,5,4,3,2:T(4,128)} reshape(f32[64,5,512]{0,2,1:T(8,128)S(1)} %copy.21) | data formatting | bytes 1310720 | tf_op jit(solution)/shard_map/gather | solution.py:96
  30.6 9.9 %select_bitcast_fusion = f32[5,8,4,8,16,8]{4,2,5,3,1,0:T(4,128)} fusion(f32[4,16,5,8,8,8]{1,0,5,4,3,2:T(4,128)} %add.137, f32[4,16,5,8,8,8]{1,0,5,4,3,2:T(4,128)} %gather.14, pred[4,16]{1,0:T(4,128)(4,1)S(1)} %eq.17), kind=kLoop, calls=%fused_computation.3 | loop fusion | flops 163840 | bytes 1966144 | tf_op jit(solution)/shard_map/transpose | solution.py:106
  40.5 9.4 %copy.22 = f32[5,8,4,8,16,8]{5,4,3,2,1,0:T(8,128)} copy(f32[5,8,4,8,16,8]{4,2,5,3,1,0:T(4,128)} %select_bitcast_fusion) | data formatting | bytes 1310720 | tf_op jit(solution)/shard_map/transpose | solution.py:106
  49.9 7.8 %reshape.102 = f32[5,8,32,128]{3,2,1,0:T(8,128)S(1)} reshape(f32[5,8,4,8,16,8]{5,4,3,2,1,0:T(8,128)} %copy.22) | data formatting | bytes 1310720 | tf_op jit(solution)/shard_map/reshape | solution.py:107
  57.8 0.0 copy-start.2
  57.8 3.2 %collective-permute-start.1 = (f32[5,2,32,128]{3,2,1,0:T(8,128)S(1)}, f32[5,2,32,128]{3,2,1,0:T(8,128)S(1)}, u32[]{:S(2)}, u32[]{:S(2)}) collective-permute-start(f32[5,2,32,128]{3,2,1,0:T(8,128)S(1)} %get-tuple-element.16), channel_id=1, source_target_pairs={{0,4},{4,8},{8,12},{12,16},{16,20},{20,24},{24,28},{1,5},{5,9},{9,... | collective-permute-start | bytes 491528 | tf_op jit(solution)/shard_map/ppermute | solution.py:21
  61.0 1.3 %collective-permute-start.2 = (f32[5,2,32,128]{3,2,1,0:T(8,128)S(1)}, f32[5,2,32,128]{3,2,1,0:T(8,128)S(1)}, u32[]{:S(2)}, u32[]{:S(2)}) collective-permute-start(f32[5,2,32,128]{3,2,1,0:T(8,128)S(1)} %get-tuple-element.15), channel_id=1, source_target_pairs={{4,0},{8,4},{12,8},{16,12},{20,16},{24,20},{28,24},{5,1},{9,5},{13... | collective-permute-start | bytes 491528 | tf_op jit(solution)/shard_map/ppermute | solution.py:24
  62.3 2.2 %collective-permute-done.1 = f32[5,2,32,128]{3,2,1,0:T(8,128)S(1)} collective-permute-done((f32[5,2,32,128]{3,2,1,0:T(8,128)S(1)}, f32[5,2,32,128]{3,2,1,0:T(8,128)S(1)}, u32[]{:S(2)}, u32[]{:S(2)}) %collective-permute-start.1) | collective-permute-done | bytes 163872 | tf_op jit(solution)/shard_map/ppermute | solution.py:21
  64.6 0.2 constant_dynamic-update-slice_fusion
  64.7 3.6 %collective-permute-done.2 = f32[5,2,32,128]{3,2,1,0:T(8,128)S(1)} collective-permute-done((f32[5,2,32,128]{3,2,1,0:T(8,128)S(1)}, f32[5,2,32,128]{3,2,1,0:T(8,128)S(1)}, u32[]{:S(2)}, u32[]{:S(2)}) %collective-permute-start.2) | collective-permute-done | bytes 163872 | tf_op jit(solution)/shard_map/ppermute | solution.py:24
  68.4 4.4 %collective-permute-start.3 = (f32[5,12,2,128]{3,2,1,0:T(2,128)S(1)}, f32[5,12,2,128]{3,2,1,0:T(2,128)S(1)}, u32[]{:S(2)}, u32[]{:S(2)}) collective-permute-start(f32[5,12,2,128]{3,2,1,0:T(2,128)S(1)} %get-tuple-element.11), channel_id=1, source_target_pairs={{0,1},{1,2},{2,3},{4,5},{5,6},{6,7},{8,9},{9,10},{10,11},{12,13},{... | collective-permute-start | bytes 184328 | tf_op jit(solution)/shard_map/ppermute | solution.py:21
  72.8 2.1 %collective-permute-start.4 = (f32[5,12,2,128]{3,2,1,0:T(2,128)S(1)}, f32[5,12,2,128]{3,2,1,0:T(2,128)S(1)}, u32[]{:S(2)}, u32[]{:S(2)}) collective-permute-start(f32[5,12,2,128]{3,2,1,0:T(2,128)S(1)} %get-tuple-element.12), channel_id=1, source_target_pairs={{1,0},{2,1},{3,2},{5,4},{6,5},{7,6},{9,8},{10,9},{11,10},{13,12},{... | collective-permute-start | bytes 184328 | tf_op jit(solution)/shard_map/ppermute | solution.py:24
  74.9 0.0 collective-permute-done.3
  74.9 3.4 %collective-permute-done.4 = f32[5,12,2,128]{3,2,1,0:T(2,128)S(1)} collective-permute-done((f32[5,12,2,128]{3,2,1,0:T(2,128)S(1)}, f32[5,12,2,128]{3,2,1,0:T(2,128)S(1)}, u32[]{:S(2)}, u32[]{:S(2)}) %collective-permute-start.4) | collective-permute-done | bytes 61472 | tf_op jit(solution)/shard_map/ppermute | solution.py:24
  78.3 1.0 %select_maximum_fusion = f32[5,12,36,132]{3,2,1,0:T(8,128)S(1)} fusion(f32[5,12,2,128]{3,2,1,0:T(2,128)S(1)} %collective-permute-done.4, f32[5,12,32,128]{3,2,1,0:T(8,128)S(1)} %constant_dynamic-update-slice_fusion.2, f32[5,12,2,128]{3,2,1,0:T(2,128)S(1)} %collective-permute-done.3), kind=kLoop, calls=%fused_computation.6 | loop fusion | flops 2280960 | bytes 2246400 | tf_op jit(solution)/shard_map/concatenate | solution.py:25
  79.3 3.9 %add_subtract_fusion = f32[5,8,32,128]{3,2,1,0:T(8,128)} fusion(f32[5,8,32,128]{3,2,1,0:T(8,128)S(1)} %reshape.102, f32[5,12,36,132]{3,2,1,0:T(8,128)S(1)} %select_maximum_fusion, f32[5,12,32,128]{3,2,1,0:T(8,128)S(1)} %constant_dynamic-update-slice_fusion.2, f32[5,12,2,128]{3,2,1,0:T(2,128)S(1)} %collective-permute-done.3, ...), kind=kLoop, calls=%fused_computation.22 | loop fusion | flops 12451840 | bytes 5857340 | tf_op jit(solution)/shard_map/sub | solution.py:79
  (21 shorter events, 0.2 us)
Async XLA Ops:
  0.0 5.9 %copy-start = (f32[64,5,512]{2,0,1:T(8,128)S(1)}, f32[64,5,512]{2,0,1:T(8,128)}, u32[]{:S(2)}) copy-start(f32[64,5,512]{2,0,1:T(8,128)} %param.7) | copy-start | bytes 1966084
  1.1 16.1 %collective-permute-start = (f32[64,5,64]{2,1,0:T(8,128)S(1)}, f32[64,5,64]{2,1,0:T(8,128)S(1)}, u32[]{:S(2)}, u32[]{:S(2)}) collective-permute-start(f32[64,5,64]{2,1,0:T(8,128)S(1)} %copy.17), channel_id=1, source_target_pairs={{0,4},{4,8},{8,12},{12,16},{16,20},{20,24},{24,28},{28,0},{1,5},{5... | collective-permute-start | bytes 245768 | tf_op jit(solution)/shard_map/ppermute | solution.py:13
  7.4 5.3 %copy-start.3 = (s32[1,1,64]{2,1,0:T(1,128)S(1)}, s32[1,1,64]{2,1,0:T(1,128)}, u32[]{:S(2)}) copy-start(s32[1,1,64]{2,1,0:T(1,128)} %param.11) | copy-start | bytes 772
  7.5 5.4 %copy-start.4 = (s32[1,1,64]{2,1,0:T(1,128)S(1)}, s32[1,1,64]{2,1,0:T(1,128)}, u32[]{:S(2)}) copy-start(s32[1,1,64]{2,1,0:T(1,128)} %param.9) | copy-start | bytes 772
  7.5 9.6 %copy-start.5 = (s32[1,1,64]{2,1,0:T(1,128)S(1)}, s32[1,1,64]{2,1,0:T(1,128)}, u32[]{:S(2)}) copy-start(s32[1,1,64]{2,1,0:T(1,128)} %param.10) | copy-start | bytes 772
  7.5 11.6 %copy-start.1 = (f32[2]{0:T(128)S(1)}, f32[2]{0:T(128)}, u32[]{:S(2)}) copy-start(f32[2]{0:T(128)} %constant.34.clone) | copy-start | bytes 28
  8.4 16.8 %all-to-all-start = ((f32[4,16,5,512]{3,1,2,0:T(8,128)}), f32[4,16,5,512]{3,1,2,0:T(8,128)S(1)}, u32[]{:S(2)}, u32[]{:S(2)}) async-start(f32[4,16,5,512]{3,1,2,0:T(8,128)} %copy.19), calls=%async_computation | async-start | bytes 1310720 | tf_op jit(solution)/shard_map/all_to_all | solution.py:91
  57.8 17.1 %copy-start.2 = (f32[3,5]{1,0:T(4,128)S(1)}, f32[3,5]{1,0:T(4,128)}, u32[]{:S(2)}) copy-start(f32[3,5]{1,0:T(4,128)} %param.12) | copy-start | bytes 184
  57.8 6.7 %collective-permute-start.1 = (f32[5,2,32,128]{3,2,1,0:T(8,128)S(1)}, f32[5,2,32,128]{3,2,1,0:T(8,128)S(1)}, u32[]{:S(2)}, u32[]{:S(2)}) collective-permute-start(f32[5,2,32,128]{3,2,1,0:T(8,128)S(1)} %get-tuple-element.16), channel_id=1, source_target_pairs={{0,4},{4,8},{8,12},{12,16},{16,20},{20,24},{24,28},{1,5},{5,9},{9,... | collective-permute-start | bytes 491528 | tf_op jit(solution)/shard_map/ppermute | solution.py:21
  61.0 7.3 %collective-permute-start.2 = (f32[5,2,32,128]{3,2,1,0:T(8,128)S(1)}, f32[5,2,32,128]{3,2,1,0:T(8,128)S(1)}, u32[]{:S(2)}, u32[]{:S(2)}) collective-permute-start(f32[5,2,32,128]{3,2,1,0:T(8,128)S(1)} %get-tuple-element.15), channel_id=1, source_target_pairs={{4,0},{8,4},{12,8},{16,12},{20,16},{24,20},{28,24},{5,1},{9,5},{13... | collective-permute-start | bytes 491528 | tf_op jit(solution)/shard_map/ppermute | solution.py:24
  68.4 6.5 %collective-permute-start.3 = (f32[5,12,2,128]{3,2,1,0:T(2,128)S(1)}, f32[5,12,2,128]{3,2,1,0:T(2,128)S(1)}, u32[]{:S(2)}, u32[]{:S(2)}) collective-permute-start(f32[5,12,2,128]{3,2,1,0:T(2,128)S(1)} %get-tuple-element.11), channel_id=1, source_target_pairs={{0,1},{1,2},{2,3},{4,5},{5,6},{6,7},{8,9},{9,10},{10,11},{12,13},{... | collective-permute-start | bytes 184328 | tf_op jit(solution)/shard_map/ppermute | solution.py:21
  72.8 5.5 %collective-permute-start.4 = (f32[5,12,2,128]{3,2,1,0:T(2,128)S(1)}, f32[5,12,2,128]{3,2,1,0:T(2,128)S(1)}, u32[]{:S(2)}, u32[]{:S(2)}) collective-permute-start(f32[5,12,2,128]{3,2,1,0:T(2,128)S(1)} %get-tuple-element.12), channel_id=1, source_target_pairs={{1,0},{2,1},{3,2},{5,4},{6,5},{7,6},{9,8},{10,9},{11,10},{13,12},{... | collective-permute-start | bytes 184328 | tf_op jit(solution)/shard_map/ppermute | solution.py:24
where the time goes:
time: 84.1 us; the launch traced here: 83.2 us
  local copies, waits for them, and re-layouts  32 us (38%)
  other arithmetic  24.2 us (29%)
  starting transfers between devices  17.4 us (21%)
  waiting for transfers between devices  9.25 us (11%)
    transpose x1, other arithmetic, local(): region = refilled.reshape(BY, BX, fields, E, E, E).transpose(2, 3, 0, 4,...  9.9 us
    transpose x1, local copies, waits for them, and re-layouts, local(): region = refilled.reshape(BY, BX, fields, E, E, E).transpose(2, 3, 0, 4,...  9.38 us
    reshape x1, local copies, waits for them, and re-layouts, local(): region = refilled.reshape(BY, BX, fields, E, E, E).transpose(2, 3, 0, 4,...  7.85 us
    ppermute x2, starting transfers between devices, with_halo(): lax.ppermute(lax.slice_in_dim(block, block.shape[dim] - width, None, axis...  7.54 us
    ppermute x2, waiting for transfers between devices, with_halo(): lax.ppermute(lax.slice_in_dim(block, 0, width, axis=dim), axis, backward)  7 us
    gather x3, local copies, waits for them, and re-layouts, local(): moved = arrived[jnp.argsort(recv_order)]  4.98 us
    add x1, local copies, waits for them, and re-layouts, refine_block(): fine = spread(cells) + offset  4.62 us
    all_to_all x1, starting transfers between devices, local(): lax.all_to_all(outgoing, 'tile', split_axis=0, concat_axis=0, tiled=True)  4.41 us
  transfers between devices with their start and end apart: 6, of which 3 were waited for; matrix products, arithmetic and copies ran while one was open for 21% of the time, Pallas kernels for 0%

commit v1 on v0

v1 whole, which is shorter than its diff:
```python
import functools

import jax
import jax.numpy as jnp
from jax import lax
from jax.experimental import pallas as pl
from jax.experimental.pallas import tpu as pltpu
from jax.sharding import PartitionSpec as P

E = 8
BX = 16
BY = 4
LANES = 128
ORDER = (3, 0, 1, 2)
MESH = pl.DeviceIdType.MESH


def minmod(a, b):
    return jnp.maximum(jnp.minimum(a, jnp.maximum(b, 0.0)), jnp.minimum(b, 0.0))


def split(x):
    high = x.astype(jnp.bfloat16)
    low = (x - high.astype(jnp.float32)).astype(jnp.bfloat16)
    return high, low


def pick(onehot2, x):
    high, low = split(x)
    return jnp.dot(onehot2, jnp.concatenate([high, low], axis=0), preferred_element_type=jnp.float32)


def iota(shape, dim):
    return lax.broadcasted_iota(jnp.int32, shape, dim)


def column(row):
    size = row.shape[1]
    diag = iota((size, size), 0) == iota((size, size), 1)
    return jnp.sum(jnp.where(diag, jnp.broadcast_to(row, (size, size)), 0.0), axis=1, keepdims=True)


def twice(onehot):
    half = jnp.where(onehot, 1.0, 0.0).astype(jnp.bfloat16)
    return jnp.concatenate([half, half], axis=1)


def refine_matrix(h):
    rows, cols = 2 * 64, 512
    i, j = iota((rows, cols), 0), iota((rows, cols), 1)
    parent = ((j >> 7) << 4) + (((j >> 4) & 3) << 2) + ((j >> 1) & 3) + h * 64
    match = jnp.where(i == parent, 1.0, 0.0)
    out = [match]
    for bit in (6, 3, 0):
        sign = jnp.where(((j >> bit) & 1) == 1, 0.25, -0.25)
        out.append(match * sign)
    return jnp.concatenate([m.astype(jnp.bfloat16) for m in out], axis=0)


def parent_slopes(c):
    lane = iota(c.shape, 1)
    out = [c]
    for bit in (4, 2, 0):
        step = 1 << bit
        inside = ((lane >> bit) & 3) != 0
        below = jnp.where(inside, c - pltpu.roll(c, step, 1), 0.0)
        above = pltpu.roll(below, LANES - step, 1)
        out.append(minmod(below, above))
    return out


def swap_lanes(rows):
    lane = iota(rows[0].shape, 1)
    rows = list(rows)
    for b in range(4):
        step = 8 << b
        upper = ((lane >> (3 + b)) & 1) == 1
        for i in range(16):
            if i & (1 << b):
                continue
            j = i | (1 << b)
            x, y = rows[i], rows[j]
            rows[i] = jnp.where(upper, pltpu.roll(y, step, 1), x)
            rows[j] = jnp.where(upper, y, pltpu.roll(x, LANES - step, 1))
    return rows


def step_x(u, c):
    lane = iota(u.shape, 1)
    first, last = lane == 0, lane == LANES - 1
    d = u - jnp.where(first, 0.0, pltpu.roll(u, 1, 1))
    above = jnp.where(last, -u, pltpu.roll(d, LANES - 1, 1))
    g = u + 0.5 * minmod(d, above)
    return c * (g - jnp.where(first, 0.0, pltpu.roll(g, 1, 1)))


def step_y(u, low2, low1, high, c):
    n = u.shape[0]
    row = iota(u.shape, 0)
    first, last = row == 0, row == n - 1
    d = u - jnp.where(first, low1, pltpu.roll(u, 1, 0))
    above = jnp.where(last, high - u, pltpu.roll(d, n - 1, 0))
    g = u + 0.5 * minmod(d, above)
    under = low1 + 0.5 * minmod(low1 - low2, d[0:1])
    return c * (g - jnp.where(first, under, pltpu.roll(g, 1, 0)))


def kernel(
    slabs, tiles, old_hbm, coarse_hbm, owner_ref, refine_ref, parent_ref, courant,
    out, old, coarse, csend, crecv, send, recv, matrix, interp, tmp, region,
    zlow, zhigh, ysend_up, ysend_down, ylow, yhigh,
    load_sem, csem, asend, arecv, zsem, ysend_sem, yrecv_sem,
):
    slab, tile = lax.axis_index("slab"), lax.axis_index("tile")
    fields, blocks, cells = old.shape
    groups = cells // LANES
    rows = BY * E
    share = blocks // tiles
    up, down = lax.rem(slab + 1, slabs), lax.rem(slab + slabs - 1, slabs)
    has_down, has_up = slab > 0, slab < slabs - 1
    has_left, has_right = tile > 0, tile < tiles - 1

    barrier = pltpu.get_barrier_semaphore()
    for s in (up, down):
        pl.semaphore_signal(barrier, inc=1, device_id={"slab": s}, device_id_type=MESH)
    for o in range(1, tiles):
        pl.semaphore_signal(
            barrier, inc=1, device_id={"tile": lax.rem(tile + o, tiles)}, device_id_type=MESH
        )
    load_old = pltpu.make_async_copy(old_hbm, old, load_sem.at[0])
    load_coarse = pltpu.make_async_copy(coarse_hbm, coarse, load_sem.at[1])
    load_coarse.start()
    load_old.start()

    offset = owner_ref[0] - tile
    offset = jnp.where(offset < 0, offset + tiles, offset).astype(jnp.float32)
    square = (blocks, blocks)
    same = column(offset) == jnp.broadcast_to(offset, square)
    earlier = iota(square, 0) < iota(square, 1)
    rank = jnp.sum(jnp.where(same & earlier, 1.0, 0.0), axis=0, keepdims=True)
    place = offset * share + rank
    pack = twice(iota(square, 0).astype(jnp.float32) == jnp.broadcast_to(place, square))
    unpack_at = column(place) == iota(square, 1).astype(jnp.float32)
    refine = column(refine_ref[0].astype(jnp.float32)) > 0.5
    unpack = twice(unpack_at & ~refine)
    parents = twice((column(parent_ref[0].astype(jnp.float32)) == iota(square, 1).astype(jnp.float32)) & refine)

    load_coarse.wait()
    for f in range(fields):
        csend[f // 2, :, (f % 2) * 64:(f % 2) * 64 + 64] = coarse[f]
    if fields % 2:
        csend[fields // 2, :, 64:] = jnp.zeros((blocks, 64), jnp.float32)

    pl.semaphore_wait(barrier, tiles + 1)
    send_coarse = pltpu.make_async_remote_copy(
        csend, crecv, csem.at[0], csem.at[1], device_id={"slab": up}, device_id_type=MESH
    )
    send_coarse.start()

    def exchange(g, o):
        return pltpu.make_async_remote_copy(
            send.at[g, :, o], recv.at[g, :, o], asend.at[g, o], arecv.at[g, o],
            device_id={"tile": lax.rem(tile + o, tiles)}, device_id_type=MESH,
        )

    load_old.wait()
    for g in ORDER:
        for f in range(fields):
            packed = pick(pack, old[f, :, g * LANES:(g + 1) * LANES])
            send[g, f] = packed.reshape(tiles, share, LANES)
            recv[g, f, 0] = packed[:share]
        for o in sorted(range(1, tiles), key=lambda o: -min(o, tiles - o)):
            exchange(g, o).start()

    @pl.when(jnp.logical_not(has_down))
    def _():
        zlow[...] = jnp.zeros_like(zlow)

    @pl.when(jnp.logical_not(has_up))
    def _():
        zhigh[...] = jnp.zeros_like(zhigh)

    @pl.when(jnp.logical_not(has_left))
    def _():
        ylow[...] = jnp.zeros_like(ylow)

    @pl.when(jnp.logical_not(has_right))
    def _():
        yhigh[...] = jnp.zeros_like(yhigh)

    for h in range(2):
        matrix[h] = refine_matrix(h)
    send_coarse.wait_recv()
    for p in range(csend.shape[0]):
        parts = [split(part) for part in parent_slopes(pick(parents, crecv[p]))]
        high = jnp.concatenate([part[0] for part in parts], axis=1)
        low = jnp.concatenate([part[1] for part in parts], axis=1)
        for h in range(2):
            if 2 * p + h < fields:
                interp[2 * p + h] = jnp.dot(
                    high, matrix[h], preferred_element_type=jnp.float32
                ) + jnp.dot(low, matrix[h], preferred_element_type=jnp.float32)

    send_up = pltpu.make_async_remote_copy(
        region.at[E - 2:E], zlow, zsem.at[0], zsem.at[1], device_id={"slab": up}, device_id_type=MESH
    )
    send_down = pltpu.make_async_remote_copy(
        region.at[0:1], zhigh, zsem.at[2], zsem.at[3], device_id={"slab": down}, device_id_type=MESH
    )

    def send_right(g):
        return pltpu.make_async_remote_copy(
            ysend_up.at[2 * g:2 * g + 2], ylow.at[2 * g:2 * g + 2], ysend_sem.at[0, g], yrecv_sem.at[0, g],
            device_id={"tile": lax.rem(tile + 1, tiles)}, device_id_type=MESH,
        )

    def send_left(g):
        return pltpu.make_async_remote_copy(
            ysend_down.at[2 * g:2 * g + 2], yhigh.at[2 * g:2 * g + 2], ysend_sem.at[1, g], yrecv_sem.at[1, g],
            device_id={"tile": lax.rem(tile + tiles - 1, tiles)}, device_id_type=MESH,
        )

    def field_rows(f):
        return pl.ds(pl.multiple_of(f * rows, rows), rows)

    for g in ORDER:
        for o in range(1, tiles):
            exchange(g, o).wait_recv()
        for f in range(fields):
            moved = pick(unpack, recv[g, f].reshape(blocks, LANES))
            tmp[g, f * blocks:(f + 1) * blocks] = moved + interp[f, :, g * LANES:(g + 1) * LANES]
        turned = swap_lanes([tmp[g, pl.ds(b, fields * BY, stride=BX), :] for b in range(BX)])
        for j in range(BX):
            region[2 * g + j // E, pl.ds(j % E, fields * BY, stride=E), :] = turned[j]
        if g == 3:
            pl.when(has_up)(send_up.start)
        if g == 0:
            pl.when(has_down)(send_down.start)
        for z in (2 * g, 2 * g + 1):
            for i in range(2):
                ysend_up[z, i] = region[z, pl.ds(rows - 2 + i, fields, stride=rows), :]
            ysend_down[z, 0] = region[z, pl.ds(0, fields, stride=rows), :]
        pl.when(has_right)(send_right(g).start)
        pl.when(has_left)(send_left(g).start)

        def along_x(f, carry, g=g):
            for z in (2 * g, 2 * g + 1):
                u = region[z, field_rows(f), :]
                out[f, z] = u - step_x(u, courant[2, f])
            return carry

        lax.fori_loop(0, fields, along_x, 0)

    def along_z(f, carry):
        c = courant[0, f]
        u = [region[z, field_rows(f), :] for z in range(E)]
        d = [None] + [u[z] - u[z - 1] for z in range(1, E)]
        g = [None] + [u[z] + 0.5 * minmod(d[z], d[z + 1]) for z in range(1, E - 1)]
        for z in range(2, E - 1):
            out[f, z] -= c * (g[z] - g[z - 1])
        return carry

    lax.fori_loop(0, fields, along_z, 0)

    for g in ORDER:
        pl.when(has_left)(send_right(g).wait_recv)
        pl.when(has_right)(send_left(g).wait_recv)

    for z in range(E):
        for f in range(fields):
            u = region[z, f * rows:(f + 1) * rows, :]
            out[f, z] -= step_y(
                u, ylow[z, 0, f:f + 1], ylow[z, 1, f:f + 1], yhigh[z, 0, f:f + 1], courant[1, f]
            )

    pl.when(has_down)(send_up.wait_recv)
    pl.when(has_up)(send_down.wait_recv)

    def edges(f, carry):
        c = courant[0, f]
        at = field_rows(f)
        u = {z: region[z, at, :] for z in (0, 1, 2, E - 3, E - 2, E - 1)}
        u[-2], u[-1], u[E] = zlow[0, at, :], zlow[1, at, :], zhigh[0, at, :]
        d = {z: u[z] - u[z - 1] for z in (-1, 0, 1, 2, E - 2, E - 1, E)}
        g = {z: u[z] + 0.5 * minmod(d[z], d[z + 1]) for z in (-1, 0, 1, E - 2, E - 1)}
        for z in (0, 1, E - 1):
            out[f, z] -= c * (g[z] - g[z - 1])
        return carry

    lax.fori_loop(0, fields, edges, 0)

    send_coarse.wait_send()
    for g in ORDER:
        for o in range(1, tiles):
            exchange(g, o).wait_send()
        pl.when(has_right)(send_right(g).wait_send)
        pl.when(has_left)(send_left(g).wait_send)
    pl.when(has_up)(send_up.wait_send)
    pl.when(has_down)(send_down.wait_send)


def local(slabs, tiles, old_fine, coarse_fine, old_owner, new_refine, parent_map, courant):
    blocks, fields, cells = old_fine.shape
    half = coarse_fine.shape[2]
    groups = cells // LANES
    share = blocks // tiles
    rows = BY * E
    pairs = -(-fields // 2)
    f32 = jnp.float32
    vmem = pl.BlockSpec(memory_space=pltpu.VMEM)
    anywhere = pl.BlockSpec(memory_space=pl.ANY)
    dma = pltpu.SemaphoreType.DMA
    return pl.pallas_call(
        functools.partial(kernel, slabs, tiles),
        out_shape=jax.ShapeDtypeStruct((fields, E, rows, BX * E), f32),
        in_specs=[anywhere, anywhere, vmem, vmem, vmem, pl.BlockSpec(memory_space=pltpu.SMEM)],
        out_specs=vmem,
        scratch_shapes=[
            pltpu.VMEM((fields, blocks, cells), f32),
            pltpu.VMEM((fields, blocks, half), f32),
            pltpu.VMEM((pairs, blocks, LANES), f32),
            pltpu.VMEM((pairs, blocks, LANES), f32),
            pltpu.VMEM((groups, fields, tiles, share, LANES), f32),
            pltpu.VMEM((groups, fields, tiles, share, LANES), f32),
            pltpu.VMEM((2, 4 * LANES, cells), jnp.bfloat16),
            pltpu.VMEM((fields, blocks, cells), f32),
            pltpu.VMEM((groups, fields * blocks, LANES), f32),
            pltpu.VMEM((E, fields * rows, LANES), f32),
            pltpu.VMEM((2, fields * rows, LANES), f32),
            pltpu.VMEM((1, fields * rows, LANES), f32),
            pltpu.VMEM((E, 2, fields, LANES), f32),
            pltpu.VMEM((E, 1, fields, LANES), f32),
            pltpu.VMEM((E, 2, fields, LANES), f32),
            pltpu.VMEM((E, 1, fields, LANES), f32),
            dma((2,)),
            dma((2,)),
            dma((groups, tiles)),
            dma((groups, tiles)),
            dma((4,)),
            dma((2, groups)),
            dma((2, groups)),
        ],
        compiler_params=pltpu.CompilerParams(
            collective_id=0, has_side_effects=True, vmem_limit_bytes=40 * 1024 * 1024
        ),
        cost_estimate=pl.CostEstimate(flops=20_000_000, bytes_accessed=2_000_000, transcendentals=0),
    )(
        jnp.transpose(old_fine, (1, 0, 2)),
        jnp.transpose(coarse_fine, (1, 0, 2)),
        old_owner,
        new_refine,
        parent_map,
        courant,
    )


def solution(mesh):
    in_specs = (
        P(("slab", "tile"), None, None),
        P(("slab", "tile"), None, None),
        P("slab", "tile", None),
        P("slab", "tile", None),
        P("slab", "tile", None),
        P(),
    )
    out_specs = P(None, "slab", "tile", None)
    body = functools.partial(local, mesh.shape["slab"], mesh.shape["tile"])
    return jax.shard_map(body, mesh=mesh, in_specs=in_specs, out_specs=out_specs, check_vma=False)
```

time: 84.1 us -> 24.8 us (0.29)
  local copies, waits for them, and re-layouts: 32 us -> 3.53 us
  other arithmetic: 24.2 us -> 0 us
  Pallas kernels: 0 us -> 21 us
  starting transfers between devices: 17.4 us -> 0 us
  waiting for transfers between devices: 9.25 us -> 0 us
    pallas_call x0 -> x1, Pallas kernels: none -> 21 us  [local(): pl.pallas_call(functools.partial(kernel, slabs, tiles), out_shape=jax.Sha...]
    ppermute x5 -> x0, starting transfers between devices: 13 us -> none  [the longest x2 7.54 us: with_halo(): lax.ppermute(lax.slice_in_dim(block, block.shape[dim] - width, None, axis...]
    transpose x1 -> x0, other arithmetic: 9.9 us -> none  [local(): region = refilled.reshape(BY, BX, fields, E, E, E).transpose(2, 3, 0, 4,...]
    transpose x1 -> x0, local copies, waits for them, and re-layouts: 9.38 us -> none  [local(): region = refilled.reshape(BY, BX, fields, E, E, E).transpose(2, 3, 0, 4,...]
    ppermute x5 -> x0, waiting for transfers between devices: 9.25 us -> none  [the longest x2 7 us: with_halo(): lax.ppermute(lax.slice_in_dim(block, 0, width, axis=dim), axis, backward)]
    reshape x2 -> x0, local copies, waits for them, and re-layouts: 8.73 us -> none  [the longest x1 7.85 us: local(): region = refilled.reshape(BY, BX, fields, E, E, E).transpose(2, 3, 0, 4,...]
    gather x6 -> x0, local copies, waits for them, and re-layouts: 7.29 us -> none  [the longest x3 4.98 us: local(): moved = arrived[jnp.argsort(recv_order)]]
    sort x3 -> x0, other arithmetic: 6.92 us -> none  [the longest x1 2.69 us: local(): send_order = jnp.argsort(owner, stable=True)]
  transfers between devices with their start and end apart: 6 -> 0, of which waited for: 3 -> 0; matrix products, arithmetic and copies ran while one was open for 21% -> 0% of each run, Pallas kernels for 0% -> 0%
where the time goes in v1:
time: 24.8 us; the launch traced here: 24.6 us
  Pallas kernels  21 us (85%)
  local copies, waits for them, and re-layouts  3.53 us (14%)
    pallas_call x1, Pallas kernels, local(): pl.pallas_call(functools.partial(kernel, slabs, tiles), out_shape=jax.Sha...  21 us
    unnamed x13, local copies, waits for them, and re-layouts  3.53 us

profile of v1, /device:TPU:1, one launch (start us, length us, event | category | flops | bytes accessed | tf_op | source)
XLA Modules:
  0.0 24.6 jit_solution(1667563588755443980)
XLA Ops:
  0.0 0.0 copy-start.2
  0.0 0.0 copy-start.3
  0.0 0.0 copy-start.4
  0.0 0.0 copy-start.5
  0.0 0.7 %copy-done.2 = f32[3,5]{1,0:T(4,128)S(1)} copy-done((f32[3,5]{1,0:T(4,128)S(1)}, f32[3,5]{1,0:T(4,128)}, u32[]{:S(2)}) %copy-start.2) | copy-done | bytes 84
  0.7 0.0 copy-done.3
  0.7 0.0 copy-done.4
  0.7 0.0 copy-done.5
  0.7 0.0 copy-start
  0.7 1.1 %copy-done = f32[64,5,512]{2,0,1:T(8,128)S(1)} copy-done((f32[64,5,512]{2,0,1:T(8,128)S(1)}, f32[64,5,512]{2,0,1:T(8,128)}, u32[]{:S(2)}) %copy-start) | copy-done | bytes 655384
  1.8 0.0 copy-start.1
  1.8 0.9 %copy-done.1 = f32[64,5,64]{2,0,1:T(8,128)S(1)} copy-done((f32[64,5,64]{2,0,1:T(8,128)S(1)}, f32[64,5,64]{2,0,1:T(8,128)}, u32[]{:S(2)}) %copy-start.1) | copy-done | bytes 81944
  2.7 21.0 %shard_map.64 = f32[5,8,32,128]{3,2,1,0:T(8,128)S(1)} custom-call(f32[5,64,512]{2,1,0:T(8,128)S(1)} %bitcast.2, f32[5,64,64]{2,1,0:T(8,128)S(1)} %bitcast.3, s32[1,1,64]{2,1,0:T(1,128)S(1)} %copy-done.3, s32[1,1,64]{2,1,0:T(1,128)S(1)} %copy-done.4, s32[1,1,64]{2,1,0:T(1,128)S(1)} %copy-done.5, f32[3,5]{1,0:T(4,128)S(1)} %copy-done.2), custom_call_target="tpu_custom_call" | custom-call | flops 20000000 | bytes 2000000 | tf_op jit(solution)/shard_map/pallas_call | solution.py:313
  23.7 0.8 %copy.8 = f32[5,8,32,128]{3,2,1,0:T(8,128)} copy(f32[5,8,32,128]{3,2,1,0:T(8,128)S(1)} %shard_map.64) | data formatting | bytes 1310720
Async XLA Ops:
  0.0 0.7 %copy-start.2 = (f32[3,5]{1,0:T(4,128)S(1)}, f32[3,5]{1,0:T(4,128)}, u32[]{:S(2)}) copy-start(f32[3,5]{1,0:T(4,128)} %courant.1) | copy-start | bytes 184
  0.0 0.7 %copy-start.3 = (s32[1,1,64]{2,1,0:T(1,128)S(1)}, s32[1,1,64]{2,1,0:T(1,128)}, u32[]{:S(2)}) copy-start(s32[1,1,64]{2,1,0:T(1,128)} %owner_ref.1) | copy-start | bytes 772
  0.0 0.7 %copy-start.4 = (s32[1,1,64]{2,1,0:T(1,128)S(1)}, s32[1,1,64]{2,1,0:T(1,128)}, u32[]{:S(2)}) copy-start(s32[1,1,64]{2,1,0:T(1,128)} %refine_ref.1) | copy-start | bytes 772
  0.0 0.7 %copy-start.5 = (s32[1,1,64]{2,1,0:T(1,128)S(1)}, s32[1,1,64]{2,1,0:T(1,128)}, u32[]{:S(2)}) copy-start(s32[1,1,64]{2,1,0:T(1,128)} %parent_ref.1) | copy-start | bytes 772
  0.7 1.1 %copy-start = (f32[64,5,512]{2,0,1:T(8,128)S(1)}, f32[64,5,512]{2,0,1:T(8,128)}, u32[]{:S(2)}) copy-start(f32[64,5,512]{2,0,1:T(8,128)} %param.6) | copy-start | bytes 1966084
  1.8 0.9 %copy-start.1 = (f32[64,5,64]{2,0,1:T(8,128)S(1)}, f32[64,5,64]{2,0,1:T(8,128)}, u32[]{:S(2)}) copy-start(f32[64,5,64]{2,0,1:T(8,128)} %param.7) | copy-start | bytes 245764

commit v2 on v1

--- a/solution.py
+++ b/solution.py
@@ -106,8 +106,8 @@
 
 
 def kernel(
-    slabs, tiles, old_hbm, coarse_hbm, owner_ref, refine_ref, parent_ref, courant,
-    out, old, coarse, csend, crecv, send, recv, matrix, interp, tmp, region,
+    slabs, tiles, old_hbm, coarse_hbm, owner_hbm, refine_hbm, parent_hbm, courant_hbm,
+    out, owner_ref, refine_ref, parent_ref, courant, old, coarse, csend, crecv, send, recv, matrix, interp, tmp, region,
     zlow, zhigh, ysend_up, ysend_down, ylow, yhigh,
     load_sem, csem, asend, arecv, zsem, ysend_sem, yrecv_sem,
 ):
@@ -127,10 +127,20 @@
         pl.semaphore_signal(
             barrier, inc=1, device_id={"tile": lax.rem(tile + o, tiles)}, device_id_type=MESH
         )
-    load_old = pltpu.make_async_copy(old_hbm, old, load_sem.at[0])
-    load_coarse = pltpu.make_async_copy(coarse_hbm, coarse, load_sem.at[1])
-    load_coarse.start()
-    load_old.start()
+    sources = (owner_hbm, refine_hbm, parent_hbm, courant_hbm, coarse_hbm)
+    targets = (owner_ref, refine_ref, parent_ref, courant, coarse)
+    loads = [pltpu.make_async_copy(a, b, load_sem.at[i]) for i, (a, b) in enumerate(zip(sources, targets))]
+    for load in loads:
+        load.start()
+
+    def load_old(g):
+        at = pl.ds(g * LANES, LANES)
+        return pltpu.make_async_copy(old_hbm.at[:, :, at], old.at[:, :, at], load_sem.at[5 + g])
+
+    for g in ORDER:
+        load_old(g).start()
+    for load in loads[:3]:
+        load.wait()
 
     offset = owner_ref[0] - tile
     offset = jnp.where(offset < 0, offset + tiles, offset).astype(jnp.float32)
@@ -145,7 +155,7 @@
     unpack = twice(unpack_at & ~refine)
     parents = twice((column(parent_ref[0].astype(jnp.float32)) == iota(square, 1).astype(jnp.float32)) & refine)
 
-    load_coarse.wait()
+    loads[4].wait()
     for f in range(fields):
         csend[f // 2, :, (f % 2) * 64:(f % 2) * 64 + 64] = coarse[f]
     if fields % 2:
@@ -163,14 +173,23 @@
             device_id={"tile": lax.rem(tile + o, tiles)}, device_id_type=MESH,
         )
 
-    load_old.wait()
-    for g in ORDER:
+    def send_group(g):
+        for o in sorted(range(1, tiles), key=lambda o: -min(o, tiles - o)):
+            exchange(g, o).start()
+
+    def sent_group(g):
+        for o in range(1, tiles):
+            exchange(g, o).wait_send()
+
+    loads[3].wait()
+    for n, g in enumerate(ORDER):
+        load_old(g).wait()
         for f in range(fields):
             packed = pick(pack, old[f, :, g * LANES:(g + 1) * LANES])
             send[g, f] = packed.reshape(tiles, share, LANES)
             recv[g, f, 0] = packed[:share]
-        for o in sorted(range(1, tiles), key=lambda o: -min(o, tiles - o)):
-            exchange(g, o).start()
+        if n < 2:
+            send_group(g)
 
     @pl.when(jnp.logical_not(has_down))
     def _():
@@ -190,6 +209,8 @@
 
     for h in range(2):
         matrix[h] = refine_matrix(h)
+    sent_group(ORDER[0])
+    send_group(ORDER[2])
     send_coarse.wait_recv()
     for p in range(csend.shape[0]):
         parts = [split(part) for part in parent_slopes(pick(parents, crecv[p]))]
@@ -201,6 +222,8 @@
                     high, matrix[h], preferred_element_type=jnp.float32
                 ) + jnp.dot(low, matrix[h], preferred_element_type=jnp.float32)
 
+    sent_group(ORDER[1])
+    send_group(ORDER[3])
     send_up = pltpu.make_async_remote_copy(
         region.at[E - 2:E], zlow, zsem.at[0], zsem.at[1], device_id={"slab": up}, device_id_type=MESH
     )
@@ -290,9 +313,9 @@
     lax.fori_loop(0, fields, edges, 0)
 
     send_coarse.wait_send()
+    sent_group(ORDER[2])
+    sent_group(ORDER[3])
     for g in ORDER:
-        for o in range(1, tiles):
-            exchange(g, o).wait_send()
         pl.when(has_right)(send_right(g).wait_send)
         pl.when(has_left)(send_left(g).wait_send)
     pl.when(has_up)(send_up.wait_send)
@@ -313,9 +336,13 @@
     return pl.pallas_call(
         functools.partial(kernel, slabs, tiles),
         out_shape=jax.ShapeDtypeStruct((fields, E, rows, BX * E), f32),
-        in_specs=[anywhere, anywhere, vmem, vmem, vmem, pl.BlockSpec(memory_space=pltpu.SMEM)],
+        in_specs=[anywhere] * 6,
         out_specs=vmem,
         scratch_shapes=[
+            pltpu.VMEM(old_owner.shape, jnp.int32),
+            pltpu.VMEM(new_refine.shape, jnp.int32),
+            pltpu.VMEM(parent_map.shape, jnp.int32),
+            pltpu.SMEM(courant.shape, f32),
             pltpu.VMEM((fields, blocks, cells), f32),
             pltpu.VMEM((fields, blocks, half), f32),
             pltpu.VMEM((pairs, blocks, LANES), f32),
@@ -332,7 +359,7 @@
             pltpu.VMEM((E, 1, fields, LANES), f32),
             pltpu.VMEM((E, 2, fields, LANES), f32),
             pltpu.VMEM((E, 1, fields, LANES), f32),
-            dma((2,)),
+            dma((5 + groups,)),
             dma((2,)),
             dma((groups, tiles)),
             dma((groups, tiles)),
@@ -341,7 +368,7 @@
             dma((2, groups)),
         ],
         compiler_params=pltpu.CompilerParams(
-            collective_id=0, has_side_effects=True, vmem_limit_bytes=40 * 1024 * 1024
+            collective_id=0, has_side_effects=True, vmem_limit_bytes=60 * 1024 * 1024
         ),
         cost_estimate=pl.CostEstimate(flops=20_000_000, bytes_accessed=2_000_000, transcendentals=0),
     )(

time: 24.8 us -> 23.7 us (0.956)
  local copies, waits for them, and re-layouts: 3.53 us -> 1.99 us
  Pallas kernels: 21 us -> 21.5 us
    unnamed x13 -> x1, local copies, waits for them, and re-layouts: 3.53 us -> 1.99 us
    pallas_call x1, Pallas kernels: 21 us -> 21.5 us  [local(): pl.pallas_call(functools.partial(kernel, slabs, tiles), out_shape=jax.Sha...]
where the time goes in v2:
time: 23.7 us; the launch traced here: 23.5 us
  Pallas kernels  21.5 us (91%)
  local copies, waits for them, and re-layouts  1.99 us (8%)
    pallas_call x1, Pallas kernels, local(): pl.pallas_call(functools.partial(kernel, slabs, tiles), out_shape=jax.Sha...  21.5 us
    unnamed x1, local copies, waits for them, and re-layouts  1.99 us

profile of v2, /device:TPU:1, one launch (start us, length us, event | category | flops | bytes accessed | tf_op | source)
XLA Modules:
  0.0 23.5 jit_solution(6174997895891834328)
XLA Ops:
  0.0 21.5 %shard_map.64 = f32[5,8,32,128]{3,2,1,0:T(8,128)} custom-call(f32[5,64,512]{2,1,0:T(8,128)} %bitcast.2, f32[5,64,64]{2,1,0:T(8,128)} %bitcast.3, s32[1,1,64]{2,1,0:T(1,128)} %owner_hbm.1, s32[1,1,64]{2,1,0:T(1,128)} %refine_hbm.1, s32[1,1,64]{2,1,0:T(1,128)} %parent_hbm.1, f32[3,5]{1,0:T(4,128)} %courant_hbm.1), custom_call_target="tpu_custom_call" | custom-call | flops 20000000 | bytes 2000000 | tf_op jit(solution)/shard_map/pallas_call | solution.py:336
  21.5 2.0 %copy.8 = f32[5,8,32,128]{3,2,1,0:T(8,128)} copy(f32[5,8,32,128]{3,2,1,0:T(8,128)} %shard_map.64) | data formatting | bytes 1310720

commit v3 on v2

--- a/solution.py
+++ b/solution.py
@@ -94,15 +94,12 @@
     return c * (g - jnp.where(first, 0.0, pltpu.roll(g, 1, 1)))
 
 
-def step_y(u, low2, low1, high, c):
+def step_y(u, c):
     n = u.shape[0]
     row = iota(u.shape, 0)
-    first, last = row == 0, row == n - 1
-    d = u - jnp.where(first, low1, pltpu.roll(u, 1, 0))
-    above = jnp.where(last, high - u, pltpu.roll(d, n - 1, 0))
-    g = u + 0.5 * minmod(d, above)
-    under = low1 + 0.5 * minmod(low1 - low2, d[0:1])
-    return c * (g - jnp.where(first, under, pltpu.roll(g, 1, 0)))
+    d = u - pltpu.roll(u, 1, 0)
+    g = u + 0.5 * minmod(d, pltpu.roll(d, n - 1, 0))
+    return jnp.where((row >= 2) & (row <= n - 2), c * (g - pltpu.roll(g, 1, 0)), 0.0)
 
 
 def kernel(
@@ -130,7 +127,7 @@
     sources = (owner_hbm, refine_hbm, parent_hbm, courant_hbm, coarse_hbm)
     targets = (owner_ref, refine_ref, parent_ref, courant, coarse)
     loads = [pltpu.make_async_copy(a, b, load_sem.at[i]) for i, (a, b) in enumerate(zip(sources, targets))]
-    for load in loads:
+    for load in loads[::-1]:
         load.start()
 
     def load_old(g):
@@ -139,9 +136,24 @@
 
     for g in ORDER:
         load_old(g).start()
-    for load in loads[:3]:
+
+    loads[4].wait()
+    for f in range(fields):
+        first = f // 2 * blocks
+        if f % 2 or f + 1 < fields:
+            csend[first:first + blocks, f % 2 * 64:f % 2 * 64 + 64] = coarse[f]
+        else:
+            csend[first:first + blocks // 2, :64] = coarse[f, :blocks // 2]
+            csend[first:first + blocks // 2, 64:] = coarse[f, blocks // 2:]
+
+    pl.semaphore_wait(barrier, tiles + 1)
+    send_coarse = pltpu.make_async_remote_copy(
+        csend, crecv, csem.at[0], csem.at[1], device_id={"slab": up}, device_id_type=MESH
+    )
+    send_coarse.start()
+
+    for load in loads[:4]:
         load.wait()
-
     offset = owner_ref[0] - tile
     offset = jnp.where(offset < 0, offset + tiles, offset).astype(jnp.float32)
     square = (blocks, blocks)
@@ -155,18 +167,6 @@
     unpack = twice(unpack_at & ~refine)
     parents = twice((column(parent_ref[0].astype(jnp.float32)) == iota(square, 1).astype(jnp.float32)) & refine)
 
-    loads[4].wait()
-    for f in range(fields):
-        csend[f // 2, :, (f % 2) * 64:(f % 2) * 64 + 64] = coarse[f]
-    if fields % 2:
-        csend[fields // 2, :, 64:] = jnp.zeros((blocks, 64), jnp.float32)
-
-    pl.semaphore_wait(barrier, tiles + 1)
-    send_coarse = pltpu.make_async_remote_copy(
-        csend, crecv, csem.at[0], csem.at[1], device_id={"slab": up}, device_id_type=MESH
-    )
-    send_coarse.start()
-
     def exchange(g, o):
         return pltpu.make_async_remote_copy(
             send.at[g, :, o], recv.at[g, :, o], asend.at[g, o], arecv.at[g, o],
@@ -181,7 +181,6 @@
         for o in range(1, tiles):
             exchange(g, o).wait_send()
 
-    loads[3].wait()
     for n, g in enumerate(ORDER):
         load_old(g).wait()
         for f in range(fields):
@@ -212,8 +211,14 @@
     sent_group(ORDER[0])
     send_group(ORDER[2])
     send_coarse.wait_recv()
-    for p in range(csend.shape[0]):
-        parts = [split(part) for part in parent_slopes(pick(parents, crecv[p]))]
+    for p in range((fields + 1) // 2):
+        first = p * blocks
+        if 2 * p + 1 < fields:
+            pair = crecv[first:first + blocks]
+        else:
+            pair = crecv[first:first + blocks // 2]
+            pair = jnp.concatenate([pair, pltpu.roll(pair, 64, 1)], axis=0)
+        parts = [split(part) for part in parent_slopes(pick(parents, pair))]
         high = jnp.concatenate([part[0] for part in parts], axis=1)
         low = jnp.concatenate([part[1] for part in parts], axis=1)
         for h in range(2):
@@ -242,6 +247,9 @@
             ysend_down.at[2 * g:2 * g + 2], yhigh.at[2 * g:2 * g + 2], ysend_sem.at[1, g], yrecv_sem.at[1, g],
             device_id={"tile": lax.rem(tile + tiles - 1, tiles)}, device_id_type=MESH,
         )
+
+    def at(f, z):
+        return pl.ds(pl.multiple_of((f * E + z) * rows, rows), rows)
 
     def field_rows(f):
         return pl.ds(pl.multiple_of(f * rows, rows), rows)
@@ -266,13 +274,13 @@
         pl.when(has_right)(send_right(g).start)
         pl.when(has_left)(send_left(g).start)
 
-        def along_x(f, carry, g=g):
+        def along_xy(f, carry, g=g):
             for z in (2 * g, 2 * g + 1):
                 u = region[z, field_rows(f), :]
-                out[f, z] = u - step_x(u, courant[2, f])
+                out[at(f, z), :] = u - step_x(u, courant[2, f]) - step_y(u, courant[1, f])
             return carry
 
-        lax.fori_loop(0, fields, along_x, 0)
+        lax.fori_loop(0, fields, along_xy, 0)
 
     def along_z(f, carry):
         c = courant[0, f]
@@ -280,7 +288,7 @@
         d = [None] + [u[z] - u[z - 1] for z in range(1, E)]
         g = [None] + [u[z] + 0.5 * minmod(d[z], d[z + 1]) for z in range(1, E - 1)]
         for z in range(2, E - 1):
-            out[f, z] -= c * (g[z] - g[z - 1])
+            out[at(f, z), :] -= c * (g[z] - g[z - 1])
         return carry
 
     lax.fori_loop(0, fields, along_z, 0)
@@ -289,25 +297,40 @@
         pl.when(has_left)(send_right(g).wait_recv)
         pl.when(has_right)(send_left(g).wait_recv)
 
+    number = iota((fields, LANES), 0)
+    c = jnp.zeros((fields, LANES), jnp.float32)
+    for f in range(fields):
+        c = jnp.where(number == f, courant[1, f], c)
+
+    def face(u, below, above):
+        return u + 0.5 * minmod(below, above)
+
     for z in range(E):
-        for f in range(fields):
-            u = region[z, f * rows:(f + 1) * rows, :]
-            out[f, z] -= step_y(
-                u, ylow[z, 0, f:f + 1], ylow[z, 1, f:f + 1], yhigh[z, 0, f:f + 1], courant[1, f]
-            )
+        u = {y: region[z, pl.ds(y % rows, fields, stride=rows), :] for y in (0, 1, 2, -3, -2, -1)}
+        low2, low1, high = ylow[z, 0], ylow[z, 1], yhigh[z, 0]
+        d0, d1 = u[0] - low1, u[1] - u[0]
+        g = {
+            -1: face(low1, low1 - low2, d0),
+            0: face(u[0], d0, d1),
+            1: face(u[1], d1, u[2] - u[1]),
+        }
+        d = u[-1] - u[-2]
+        g[rows - 2], g[rows - 1] = face(u[-2], u[-2] - u[-3], d), face(u[-1], d, high - u[-1])
+        for y in (0, 1, rows - 1):
+            out[pl.ds(z * rows + y, fields, stride=E * rows), :] -= c * (g[y] - g[y - 1])
 
     pl.when(has_down)(send_up.wait_recv)
     pl.when(has_up)(send_down.wait_recv)
 
     def edges(f, carry):
         c = courant[0, f]
-        at = field_rows(f)
-        u = {z: region[z, at, :] for z in (0, 1, 2, E - 3, E - 2, E - 1)}
-        u[-2], u[-1], u[E] = zlow[0, at, :], zlow[1, at, :], zhigh[0, at, :]
+        here = field_rows(f)
+        u = {z: region[z, here, :] for z in (0, 1, 2, E - 3, E - 2, E - 1)}
+        u[-2], u[-1], u[E] = zlow[0, here, :], zlow[1, here, :], zhigh[0, here, :]
         d = {z: u[z] - u[z - 1] for z in (-1, 0, 1, 2, E - 2, E - 1, E)}
         g = {z: u[z] + 0.5 * minmod(d[z], d[z + 1]) for z in (-1, 0, 1, E - 2, E - 1)}
         for z in (0, 1, E - 1):
-            out[f, z] -= c * (g[z] - g[z - 1])
+            out[at(f, z), :] -= c * (g[z] - g[z - 1])
         return carry
 
     lax.fori_loop(0, fields, edges, 0)
@@ -328,15 +351,22 @@
     groups = cells // LANES
     share = blocks // tiles
     rows = BY * E
-    pairs = -(-fields // 2)
     f32 = jnp.float32
     vmem = pl.BlockSpec(memory_space=pltpu.VMEM)
-    anywhere = pl.BlockSpec(memory_space=pl.ANY)
+    hbm = pl.BlockSpec(memory_space=pltpu.HBM)
     dma = pltpu.SemaphoreType.DMA
-    return pl.pallas_call(
+    operands = (
+        jnp.transpose(old_fine, (1, 0, 2)),
+        jnp.transpose(coarse_fine, (1, 0, 2)),
+        old_owner,
+        new_refine,
+        parent_map,
+        courant,
+    )
+    stepped = pl.pallas_call(
         functools.partial(kernel, slabs, tiles),
-        out_shape=jax.ShapeDtypeStruct((fields, E, rows, BX * E), f32),
-        in_specs=[anywhere] * 6,
+        out_shape=pltpu.VMEM((fields * E * rows, BX * E), f32),
+        in_specs=[hbm] * 6,
         out_specs=vmem,
         scratch_shapes=[
             pltpu.VMEM(old_owner.shape, jnp.int32),
@@ -345,8 +375,8 @@
             pltpu.SMEM(courant.shape, f32),
             pltpu.VMEM((fields, blocks, cells), f32),
             pltpu.VMEM((fields, blocks, half), f32),
-            pltpu.VMEM((pairs, blocks, LANES), f32),
-            pltpu.VMEM((pairs, blocks, LANES), f32),
+            pltpu.VMEM((fields * blocks // 2, LANES), f32),
+            pltpu.VMEM((fields * blocks // 2, LANES), f32),
             pltpu.VMEM((groups, fields, tiles, share, LANES), f32),
             pltpu.VMEM((groups, fields, tiles, share, LANES), f32),
             pltpu.VMEM((2, 4 * LANES, cells), jnp.bfloat16),
@@ -368,17 +398,11 @@
             dma((2, groups)),
         ],
         compiler_params=pltpu.CompilerParams(
-            collective_id=0, has_side_effects=True, vmem_limit_bytes=60 * 1024 * 1024
+            collective_id=0, has_side_effects=True, vmem_limit_bytes=32 * 1024 * 1024
         ),
         cost_estimate=pl.CostEstimate(flops=20_000_000, bytes_accessed=2_000_000, transcendentals=0),
-    )(
-        jnp.transpose(old_fine, (1, 0, 2)),
-        jnp.transpose(coarse_fine, (1, 0, 2)),
-        old_owner,
-        new_refine,
-        parent_map,
-        courant,
-    )
+    )(*(pltpu.with_memory_space_constraint(operand, pltpu.HBM) for operand in operands))
+    return stepped.reshape(fields, E, rows, BX * E)
 
 
 def solution(mesh):

time: 23.7 us -> 21.1 us (0.89)
  Pallas kernels: 21.5 us -> 20.1 us
  local copies, waits for them, and re-layouts: 1.99 us -> 0.84 us
    pallas_call x1, Pallas kernels: 21.5 us -> 20.1 us  [local(): pl.pallas_call(functools.partial(kernel, slabs, tiles), out_shape=pltpu.V...]
    unnamed x1, local copies, waits for them, and re-layouts: 1.99 us -> 0.84 us
where the time goes in v3:
time: 21.1 us; the launch traced here: 20.9 us
  Pallas kernels  20.1 us (95%)
  local copies, waits for them, and re-layouts  0.84 us (4%)
    pallas_call x1, Pallas kernels, local(): pl.pallas_call(functools.partial(kernel, slabs, tiles), out_shape=pltpu.V...  20.1 us
    unnamed x1, local copies, waits for them, and re-layouts  0.84 us

profile of v3, /device:TPU:1, one launch (start us, length us, event | category | flops | bytes accessed | tf_op | source)
XLA Modules:
  0.0 20.9 jit_solution(5221027130352612347)
XLA Ops:
  0.0 20.1 %shard_map.64 = f32[1280,128]{1,0:T(8,128)S(1)} custom-call(f32[5,64,512]{2,1,0:T(8,128)} %bitcast.4, f32[5,64,64]{2,1,0:T(8,128)} %bitcast.5, s32[1,1,64]{2,1,0:T(1,128)} %owner_hbm.1, s32[1,1,64]{2,1,0:T(1,128)} %refine_hbm.1, s32[1,1,64]{2,1,0:T(1,128)} %parent_hbm.1, f32[3,5]{1,0:T(4,128)} %courant_hbm.1), custom_call_target="tpu_custom_call" | custom-call | flops 20000000 | bytes 2000000 | tf_op jit(solution)/shard_map/pallas_call | solution.py:366
  20.1 0.8 %copy.8 = f32[5,8,32,128]{3,2,1,0:T(8,128)} copy(f32[5,8,32,128]{3,2,1,0:T(8,128)S(1)} %bitcast.3) | data formatting | bytes 1310720

commit v4 on v3

--- a/solution.py
+++ b/solution.py
@@ -118,16 +118,20 @@
     has_left, has_right = tile > 0, tile < tiles - 1
 
     barrier = pltpu.get_barrier_semaphore()
-    for s in (up, down):
-        pl.semaphore_signal(barrier, inc=1, device_id={"slab": s}, device_id_type=MESH)
+    pl.semaphore_signal(barrier, inc=1, device_id={"slab": down}, device_id_type=MESH)
+
+    @pl.when(has_up)
+    def _():
+        pl.semaphore_signal(barrier, inc=1, device_id={"slab": up}, device_id_type=MESH)
+
     for o in range(1, tiles):
         pl.semaphore_signal(
             barrier, inc=1, device_id={"tile": lax.rem(tile + o, tiles)}, device_id_type=MESH
         )
-    sources = (owner_hbm, refine_hbm, parent_hbm, courant_hbm, coarse_hbm)
-    targets = (owner_ref, refine_ref, parent_ref, courant, coarse)
+    sources = (owner_hbm, coarse_hbm, refine_hbm, parent_hbm, courant_hbm)
+    targets = (owner_ref, coarse, refine_ref, parent_ref, courant)
     loads = [pltpu.make_async_copy(a, b, load_sem.at[i]) for i, (a, b) in enumerate(zip(sources, targets))]
-    for load in loads[::-1]:
+    for load in loads:
         load.start()
 
     def load_old(g):
@@ -137,23 +141,7 @@
     for g in ORDER:
         load_old(g).start()
 
-    loads[4].wait()
-    for f in range(fields):
-        first = f // 2 * blocks
-        if f % 2 or f + 1 < fields:
-            csend[first:first + blocks, f % 2 * 64:f % 2 * 64 + 64] = coarse[f]
-        else:
-            csend[first:first + blocks // 2, :64] = coarse[f, :blocks // 2]
-            csend[first:first + blocks // 2, 64:] = coarse[f, blocks // 2:]
-
-    pl.semaphore_wait(barrier, tiles + 1)
-    send_coarse = pltpu.make_async_remote_copy(
-        csend, crecv, csem.at[0], csem.at[1], device_id={"slab": up}, device_id_type=MESH
-    )
-    send_coarse.start()
-
-    for load in loads[:4]:
-        load.wait()
+    loads[0].wait()
     offset = owner_ref[0] - tile
     offset = jnp.where(offset < 0, offset + tiles, offset).astype(jnp.float32)
     square = (blocks, blocks)
@@ -162,10 +150,21 @@
     rank = jnp.sum(jnp.where(same & earlier, 1.0, 0.0), axis=0, keepdims=True)
     place = offset * share + rank
     pack = twice(iota(square, 0).astype(jnp.float32) == jnp.broadcast_to(place, square))
-    unpack_at = column(place) == iota(square, 1).astype(jnp.float32)
-    refine = column(refine_ref[0].astype(jnp.float32)) > 0.5
-    unpack = twice(unpack_at & ~refine)
-    parents = twice((column(parent_ref[0].astype(jnp.float32)) == iota(square, 1).astype(jnp.float32)) & refine)
+    loads[1].wait()
+    for f in range(fields):
+        first = f // 2 * blocks
+        if f % 2 or f + 1 < fields:
+            csend[first:first + blocks, f % 2 * 64:f % 2 * 64 + 64] = coarse[f]
+        else:
+            csend[first:first + blocks // 2, :64] = coarse[f, :blocks // 2]
+            csend[first:first + blocks // 2, 64:] = coarse[f, blocks // 2:]
+
+    pl.semaphore_wait(barrier, tiles + jnp.minimum(slab, 1))
+
+    send_coarse = pltpu.make_async_remote_copy(
+        csend, crecv, csem.at[0], csem.at[1], device_id={"slab": up}, device_id_type=MESH
+    )
+    send_coarse.start()
 
     def exchange(g, o):
         return pltpu.make_async_remote_copy(
@@ -206,6 +205,12 @@
     def _():
         yhigh[...] = jnp.zeros_like(yhigh)
 
+    for load in loads[2:]:
+        load.wait()
+    unpack_at = column(place) == iota(square, 1).astype(jnp.float32)
+    refine = column(refine_ref[0].astype(jnp.float32)) > 0.5
+    unpack = twice(unpack_at & ~refine)
+    parents = twice((column(parent_ref[0].astype(jnp.float32)) == iota(square, 1).astype(jnp.float32)) & refine)
     for h in range(2):
         matrix[h] = refine_matrix(h)
     sent_group(ORDER[0])

time: 21.1 us -> 21.1 us (level)
  no operation moved by 1% of the time
where the time goes in v4:
time: 21.1 us; the launch traced here: 20.9 us
  Pallas kernels  20.1 us (95%)
  local copies, waits for them, and re-layouts  0.84 us (4%)
    pallas_call x1, Pallas kernels, local(): pl.pallas_call(functools.partial(kernel, slabs, tiles), out_shape=pltpu.V...  20.1 us
    unnamed x1, local copies, waits for them, and re-layouts  0.84 us

profile of v4, /device:TPU:1, one launch (start us, length us, event | category | flops | bytes accessed | tf_op | source)
XLA Modules:
  0.0 20.9 jit_solution(5236387191498411340)
XLA Ops:
  0.0 20.1 %shard_map.64 = f32[1280,128]{1,0:T(8,128)S(1)} custom-call(f32[5,64,512]{2,1,0:T(8,128)} %bitcast.4, f32[5,64,64]{2,1,0:T(8,128)} %bitcast.5, s32[1,1,64]{2,1,0:T(1,128)} %owner_hbm.1, s32[1,1,64]{2,1,0:T(1,128)} %refine_hbm.1, s32[1,1,64]{2,1,0:T(1,128)} %parent_hbm.1, f32[3,5]{1,0:T(4,128)} %courant_hbm.1), custom_call_target="tpu_custom_call" | custom-call | flops 20000000 | bytes 2000000 | tf_op jit(solution)/shard_map/pallas_call | solution.py:371
  20.1 0.8 %copy.8 = f32[5,8,32,128]{3,2,1,0:T(8,128)} copy(f32[5,8,32,128]{3,2,1,0:T(8,128)S(1)} %bitcast.3) | data formatting | bytes 1310720

commit v5 on v4

--- a/solution.py
+++ b/solution.py
@@ -215,6 +215,7 @@
         matrix[h] = refine_matrix(h)
     sent_group(ORDER[0])
     send_group(ORDER[2])
+    send_group(ORDER[3])
     send_coarse.wait_recv()
     for p in range((fields + 1) // 2):
         first = p * blocks
@@ -232,8 +233,6 @@
                     high, matrix[h], preferred_element_type=jnp.float32
                 ) + jnp.dot(low, matrix[h], preferred_element_type=jnp.float32)
 
-    sent_group(ORDER[1])
-    send_group(ORDER[3])
     send_up = pltpu.make_async_remote_copy(
         region.at[E - 2:E], zlow, zsem.at[0], zsem.at[1], device_id={"slab": up}, device_id_type=MESH
     )
@@ -285,7 +284,7 @@
                 out[at(f, z), :] = u - step_x(u, courant[2, f]) - step_y(u, courant[1, f])
             return carry
 
-        lax.fori_loop(0, fields, along_xy, 0)
+        lax.fori_loop(0, fields, along_xy, 0, unroll=True)
 
     def along_z(f, carry):
         c = courant[0, f]
@@ -296,7 +295,7 @@
             out[at(f, z), :] -= c * (g[z] - g[z - 1])
         return carry
 
-    lax.fori_loop(0, fields, along_z, 0)
+    lax.fori_loop(0, fields, along_z, 0, unroll=True)
 
     for g in ORDER:
         pl.when(has_left)(send_right(g).wait_recv)
@@ -338,11 +337,11 @@
             out[at(f, z), :] -= c * (g[z] - g[z - 1])
         return carry
 
-    lax.fori_loop(0, fields, edges, 0)
+    lax.fori_loop(0, fields, edges, 0, unroll=True)
 
     send_coarse.wait_send()
-    sent_group(ORDER[2])
-    sent_group(ORDER[3])
+    for g in ORDER[1:]:
+        sent_group(g)
     for g in ORDER:
         pl.when(has_right)(send_right(g).wait_send)
         pl.when(has_left)(send_left(g).wait_send)

time: 21.1 us -> 18.5 us (0.88)
  Pallas kernels: 20.1 us -> 17.5 us
    pallas_call x1, Pallas kernels: 20.1 us -> 17.5 us  [local(): pl.pallas_call(functools.partial(kernel, slabs, tiles), out_shape=pltpu.V...]
where the time goes in v5:
time: 18.5 us; the launch traced here: 18.4 us
  Pallas kernels  17.5 us (95%)
  local copies, waits for them, and re-layouts  0.84 us (5%)
    pallas_call x1, Pallas kernels, local(): pl.pallas_call(functools.partial(kernel, slabs, tiles), out_shape=pltpu.V...  17.5 us
    unnamed x1, local copies, waits for them, and re-layouts  0.84 us

profile of v5, /device:TPU:1, one launch (start us, length us, event | category | flops | bytes accessed | tf_op | source)
XLA Modules:
  0.0 18.4 jit_solution(15524860508562084392)
XLA Ops:
  0.0 17.5 %shard_map.64 = f32[1280,128]{1,0:T(8,128)S(1)} custom-call(f32[5,64,512]{2,1,0:T(8,128)} %bitcast.4, f32[5,64,64]{2,1,0:T(8,128)} %bitcast.5, s32[1,1,64]{2,1,0:T(1,128)} %owner_hbm.1, s32[1,1,64]{2,1,0:T(1,128)} %refine_hbm.1, s32[1,1,64]{2,1,0:T(1,128)} %parent_hbm.1, f32[3,5]{1,0:T(4,128)} %courant_hbm.1), custom_call_target="tpu_custom_call" | custom-call | flops 20000000 | bytes 2000000 | tf_op jit(solution)/shard_map/pallas_call | solution.py:370
  17.5 0.8 %copy.8 = f32[5,8,32,128]{3,2,1,0:T(8,128)} copy(f32[5,8,32,128]{3,2,1,0:T(8,128)S(1)} %bitcast.3) | data formatting | bytes 1310720

commit v6 on v5

--- a/solution.py
+++ b/solution.py
@@ -104,7 +104,7 @@
 
 def kernel(
     slabs, tiles, old_hbm, coarse_hbm, owner_hbm, refine_hbm, parent_hbm, courant_hbm,
-    out, owner_ref, refine_ref, parent_ref, courant, old, coarse, csend, crecv, send, recv, matrix, interp, tmp, region,
+    out, owner_ref, refine_ref, parent_ref, courant, old, coarse, csend, crecv, send, recv, matrix, stacked, interp, tmp, region,
     zlow, zhigh, ysend_up, ysend_down, ylow, yhigh,
     load_sem, csem, asend, arecv, zsem, ysend_sem, yrecv_sem,
 ):
@@ -225,13 +225,21 @@
             pair = crecv[first:first + blocks // 2]
             pair = jnp.concatenate([pair, pltpu.roll(pair, 64, 1)], axis=0)
         parts = [split(part) for part in parent_slopes(pick(parents, pair))]
-        high = jnp.concatenate([part[0] for part in parts], axis=1)
-        low = jnp.concatenate([part[1] for part in parts], axis=1)
+        for n in range(2):
+            part = jnp.concatenate([part[n] for part in parts], axis=1)
+            at = (2 * p + n) * blocks
+            stacked[at:at + blocks] = part
+
+    def refined(g):
+        columns = slice(g * LANES, (g + 1) * LANES)
         for h in range(2):
-            if 2 * p + h < fields:
-                interp[2 * p + h] = jnp.dot(
-                    high, matrix[h], preferred_element_type=jnp.float32
-                ) + jnp.dot(low, matrix[h], preferred_element_type=jnp.float32)
+            count = (fields + 1 - h) // 2
+            both = jnp.dot(
+                stacked[:2 * count * blocks], matrix[h, :, columns], preferred_element_type=jnp.float32
+            )
+            for p in range(count):
+                at = 2 * p * blocks
+                interp[g, 2 * p + h] = both[at:at + blocks] + both[at + blocks:at + 2 * blocks]
 
     send_up = pltpu.make_async_remote_copy(
         region.at[E - 2:E], zlow, zsem.at[0], zsem.at[1], device_id={"slab": up}, device_id_type=MESH
@@ -259,11 +267,12 @@
         return pl.ds(pl.multiple_of(f * rows, rows), rows)
 
     for g in ORDER:
+        refined(g)
         for o in range(1, tiles):
             exchange(g, o).wait_recv()
         for f in range(fields):
             moved = pick(unpack, recv[g, f].reshape(blocks, LANES))
-            tmp[g, f * blocks:(f + 1) * blocks] = moved + interp[f, :, g * LANES:(g + 1) * LANES]
+            tmp[g, f * blocks:(f + 1) * blocks] = moved + interp[g, f]
         turned = swap_lanes([tmp[g, pl.ds(b, fields * BY, stride=BX), :] for b in range(BX)])
         for j in range(BX):
             region[2 * g + j // E, pl.ds(j % E, fields * BY, stride=E), :] = turned[j]
@@ -384,7 +393,8 @@
             pltpu.VMEM((groups, fields, tiles, share, LANES), f32),
             pltpu.VMEM((groups, fields, tiles, share, LANES), f32),
             pltpu.VMEM((2, 4 * LANES, cells), jnp.bfloat16),
-            pltpu.VMEM((fields, blocks, cells), f32),
+            pltpu.VMEM(((fields + 1) // 2 * 2 * blocks, 4 * LANES), jnp.bfloat16),
+            pltpu.VMEM((groups, fields, blocks, LANES), f32),
             pltpu.VMEM((groups, fields * blocks, LANES), f32),
             pltpu.VMEM((E, fields * rows, LANES), f32),
             pltpu.VMEM((2, fields * rows, LANES), f32),

time: 18.5 us -> 18.3 us (0.989)
  the two profiles are of different devices: /device:TPU:1 before, /device:TPU:0 now
where the time goes in v6:
time: 18.3 us; the launch traced here: 18.1 us
  Pallas kernels  17.3 us (95%)
  local copies, waits for them, and re-layouts  0.84 us (5%)
    pallas_call x1, Pallas kernels, local(): pl.pallas_call(functools.partial(kernel, slabs, tiles), out_shape=pltpu.V...  17.3 us
    unnamed x1, local copies, waits for them, and re-layouts  0.84 us

profile of v6, /device:TPU:0, one launch (start us, length us, event | category | flops | bytes accessed | tf_op | source)
XLA Modules:
  0.0 18.1 jit_solution(9943622903463725120)
XLA Ops:
  0.0 17.3 %shard_map.64 = f32[1280,128]{1,0:T(8,128)S(1)} custom-call(f32[5,64,512]{2,1,0:T(8,128)} %bitcast.4, f32[5,64,64]{2,1,0:T(8,128)} %bitcast.5, s32[1,1,64]{2,1,0:T(1,128)} %owner_hbm.1, s32[1,1,64]{2,1,0:T(1,128)} %refine_hbm.1, s32[1,1,64]{2,1,0:T(1,128)} %parent_hbm.1, f32[3,5]{1,0:T(4,128)} %courant_hbm.1), custom_call_target="tpu_custom_call" | custom-call | flops 20000000 | bytes 2000000 | tf_op jit(solution)/shard_map/pallas_call | solution.py:379
  17.3 0.8 %copy.8 = f32[5,8,32,128]{3,2,1,0:T(8,128)} copy(f32[5,8,32,128]{3,2,1,0:T(8,128)S(1)} %bitcast.3) | data formatting | bytes 1310720

commit v7 on v6

--- a/solution.py
+++ b/solution.py
@@ -186,7 +186,7 @@
             packed = pick(pack, old[f, :, g * LANES:(g + 1) * LANES])
             send[g, f] = packed.reshape(tiles, share, LANES)
             recv[g, f, 0] = packed[:share]
-        if n < 2:
+        if n == 0:
             send_group(g)
 
     @pl.when(jnp.logical_not(has_down))
@@ -214,8 +214,8 @@
     for h in range(2):
         matrix[h] = refine_matrix(h)
     sent_group(ORDER[0])
+    send_group(ORDER[1])
     send_group(ORDER[2])
-    send_group(ORDER[3])
     send_coarse.wait_recv()
     for p in range((fields + 1) // 2):
         first = p * blocks
@@ -278,6 +278,7 @@
             region[2 * g + j // E, pl.ds(j % E, fields * BY, stride=E), :] = turned[j]
         if g == 3:
             pl.when(has_up)(send_up.start)
+            send_group(ORDER[3])
         if g == 0:
             pl.when(has_down)(send_down.start)
         for z in (2 * g, 2 * g + 1):

time: 18.3 us -> 18.9 us (1.033)
  the two profiles are of different devices: /device:TPU:0 before, /device:TPU:1 now
where the time goes in v7:
time: 18.9 us; the launch traced here: 18.8 us
  Pallas kernels  17.9 us (95%)
  local copies, waits for them, and re-layouts  0.84 us (4%)
    pallas_call x1, Pallas kernels, local(): pl.pallas_call(functools.partial(kernel, slabs, tiles), out_shape=pltpu.V...  17.9 us
    unnamed x1, local copies, waits for them, and re-layouts  0.84 us

profile of v7, /device:TPU:1, one launch (start us, length us, event | category | flops | bytes accessed | tf_op | source)
XLA Modules:
  0.0 18.8 jit_solution(5656991509665057739)
XLA Ops:
  0.0 17.9 %shard_map.64 = f32[1280,128]{1,0:T(8,128)S(1)} custom-call(f32[5,64,512]{2,1,0:T(8,128)} %bitcast.4, f32[5,64,64]{2,1,0:T(8,128)} %bitcast.5, s32[1,1,64]{2,1,0:T(1,128)} %owner_hbm.1, s32[1,1,64]{2,1,0:T(1,128)} %refine_hbm.1, s32[1,1,64]{2,1,0:T(1,128)} %parent_hbm.1, f32[3,5]{1,0:T(4,128)} %courant_hbm.1), custom_call_target="tpu_custom_call" | custom-call | flops 20000000 | bytes 2000000 | tf_op jit(solution)/shard_map/pallas_call | solution.py:380
  18.0 0.8 %copy.8 = f32[5,8,32,128]{3,2,1,0:T(8,128)} copy(f32[5,8,32,128]{3,2,1,0:T(8,128)S(1)} %bitcast.3) | data formatting | bytes 1310720

commit v8 on v7

--- a/solution.py
+++ b/solution.py
@@ -216,6 +216,7 @@
     sent_group(ORDER[0])
     send_group(ORDER[1])
     send_group(ORDER[2])
+    pl.when(jnp.logical_not(has_down))(lambda: send_group(ORDER[3]))
     send_coarse.wait_recv()
     for p in range((fields + 1) // 2):
         first = p * blocks
@@ -278,7 +279,7 @@
             region[2 * g + j // E, pl.ds(j % E, fields * BY, stride=E), :] = turned[j]
         if g == 3:
             pl.when(has_up)(send_up.start)
-            send_group(ORDER[3])
+            pl.when(has_down)(lambda: send_group(ORDER[3]))
         if g == 0:
             pl.when(has_down)(send_down.start)
         for z in (2 * g, 2 * g + 1):

time: 18.9 us -> 18.4 us (0.974)
  the two profiles are of different devices: /device:TPU:1 before, /device:TPU:0 now
where the time goes in v8:
time: 18.4 us; the launch traced here: 18.2 us
  Pallas kernels  17.4 us (95%)
  local copies, waits for them, and re-layouts  0.84 us (5%)
    pallas_call x1, Pallas kernels, local(): pl.pallas_call(functools.partial(kernel, slabs, tiles), out_shape=pltpu.V...  17.4 us
    unnamed x1, local copies, waits for them, and re-layouts  0.84 us

profile of v8, /device:TPU:0, one launch (start us, length us, event | category | flops | bytes accessed | tf_op | source)
XLA Modules:
  0.0 18.2 jit_solution(13830206729797935709)
XLA Ops:
  0.0 17.4 %shard_map.64 = f32[1280,128]{1,0:T(8,128)S(1)} custom-call(f32[5,64,512]{2,1,0:T(8,128)} %bitcast.4, f32[5,64,64]{2,1,0:T(8,128)} %bitcast.5, s32[1,1,64]{2,1,0:T(1,128)} %owner_hbm.1, s32[1,1,64]{2,1,0:T(1,128)} %refine_hbm.1, s32[1,1,64]{2,1,0:T(1,128)} %parent_hbm.1, f32[3,5]{1,0:T(4,128)} %courant_hbm.1), custom_call_target="tpu_custom_call" | custom-call | flops 20000000 | bytes 2000000 | tf_op jit(solution)/shard_map/pallas_call | solution.py:381
  17.4 0.8 %copy.8 = f32[5,8,32,128]{3,2,1,0:T(8,128)} copy(f32[5,8,32,128]{3,2,1,0:T(8,128)S(1)} %bitcast.3) | data formatting | bytes 1310720

commit v9 on v7

--- a/solution.py
+++ b/solution.py
@@ -216,6 +216,7 @@
     sent_group(ORDER[0])
     send_group(ORDER[1])
     send_group(ORDER[2])
+    send_group(ORDER[3])
     send_coarse.wait_recv()
     for p in range((fields + 1) // 2):
         first = p * blocks
@@ -278,7 +279,6 @@
             region[2 * g + j // E, pl.ds(j % E, fields * BY, stride=E), :] = turned[j]
         if g == 3:
             pl.when(has_up)(send_up.start)
-            send_group(ORDER[3])
         if g == 0:
             pl.when(has_down)(send_down.start)
         for z in (2 * g, 2 * g + 1):

time: 18.9 us -> 18.4 us (0.974)
  the two profiles are of different devices: /device:TPU:1 before, /device:TPU:0 now
where the time goes in v9:
time: 18.4 us; the launch traced here: 18.2 us
  Pallas kernels  17.4 us (95%)
  local copies, waits for them, and re-layouts  0.84 us (5%)
    pallas_call x1, Pallas kernels, local(): pl.pallas_call(functools.partial(kernel, slabs, tiles), out_shape=pltpu.V...  17.4 us
    unnamed x1, local copies, waits for them, and re-layouts  0.84 us

profile of v9, /device:TPU:0, one launch (start us, length us, event | category | flops | bytes accessed | tf_op | source)
XLA Modules:
  0.0 18.2 jit_solution(8162047443585160697)
XLA Ops:
  0.0 17.4 %shard_map.64 = f32[1280,128]{1,0:T(8,128)S(1)} custom-call(f32[5,64,512]{2,1,0:T(8,128)} %bitcast.4, f32[5,64,64]{2,1,0:T(8,128)} %bitcast.5, s32[1,1,64]{2,1,0:T(1,128)} %owner_hbm.1, s32[1,1,64]{2,1,0:T(1,128)} %refine_hbm.1, s32[1,1,64]{2,1,0:T(1,128)} %parent_hbm.1, f32[3,5]{1,0:T(4,128)} %courant_hbm.1), custom_call_target="tpu_custom_call" | custom-call | flops 20000000 | bytes 2000000 | tf_op jit(solution)/shard_map/pallas_call | solution.py:380
  17.4 0.8 %copy.8 = f32[5,8,32,128]{3,2,1,0:T(8,128)} copy(f32[5,8,32,128]{3,2,1,0:T(8,128)S(1)} %bitcast.3) | data formatting | bytes 1310720
